TPU v7x, 32 devices: a whole 2x2x4 slice. The times are simulated.
32 devices in a mesh: dom: 8 (over y, x, core), blk: 4 (over z).
Axes of the slice: x: 2, y: 2, z: 4, core: 2. Of those that a mesh axis runs over, the one named last changes fastest.
Arguments:
- features: bfloat16 [32768, 128], P(('dom', 'blk')), may hold values from -6 to 6
- tile_vals: bfloat16 [2304, 128, 128], P(('dom', 'blk')), may hold values from -0.25 to 0.25
- tile_rows: int32 [32, 72], P(('dom', 'blk')), may hold values from 0 to 7
- tile_cols: int32 [32, 72], P(('dom', 'blk')), may hold values from 0 to 7
- tile_count: int32 [32, 4], P(('dom', 'blk')), may hold values from 1 to 18, as said below
- cut_weights: bfloat16 [32768, 384], P(('dom', 'blk')), may hold values from -0.4375 to 0.4375
- send_idx: int32 [32, 384], P(('dom', 'blk')), may hold values from 0 to 1023
- send_count: int32 [32, 8], P(('dom', 'blk')), may hold values from 0 to 48, as said below
- weight: bfloat16 [128, 256], replicated, may hold values from -0.5 to 0.5
- bias: float32 [256], replicated, may hold values from -3 to 3
- cotangent: bfloat16 [32768, 256], P(('dom', 'blk')), may hold values from -6 to 6
Outputs:
- out_y: bfloat16 [32768, 256], P(('dom', 'blk'))
- grad_x: bfloat16 [32768, 128], P(('dom', 'blk'))
- grad_w: float32 [128, 256], replicated
- grad_b: float32 [256], replicated
Inputs may be any that keep to these rules, and one draw needn't show every extreme that they name: `tile_count`: every device has a source position with exactly 18 live slots; devices differ strongly in their counts. `send_count`: zero toward a device's own group; at each index along blk some group receives exactly 48 rows from every other group.
All inputs are finite; a program needn't handle non-finite values.
Results may differ from a plain program's by a relative error of at most 0.018.
Values may be sent and summed in bfloat16 or wider, within the bound.
A program may use at most 128 MiB of HBM per device.

v0:
```python
import math
import jax
import jax.numpy as jnp
from jax import lax
from jax.sharding import PartitionSpec as P


def pad_piece(piece, tile_side):
    padding = jnp.zeros((tile_side, piece.shape[1]), piece.dtype)
    return jnp.concatenate([padding, piece, padding], axis=0)


def pick_blocks(padded, piece_rows, first_rows, tile_side):
    places = jnp.clip(first_rows + tile_side, 0, piece_rows + tile_side)
    picked = jax.vmap(lambda where_at: lax.dynamic_slice_in_dim(padded, where_at, tile_side, 0))(
        places
    )
    inside = (first_rows > -tile_side) & (first_rows < piece_rows)
    return (picked, inside)


def accumulate(running, tiles_here, picked, target, live, flipped):
    row_blocks = running.shape[0]
    selector = (
        (target[:, None] == jnp.arange(row_blocks, dtype=jnp.int32)[None, :]) & live[:, None]
    ).astype(tiles_here.dtype)
    pattern = "tr,tji,tjf->rif" if flipped else "tr,tij,tjf->rif"
    return running + jnp.einsum(
        pattern, selector, tiles_here, picked, preferred_element_type=jnp.float32
    )


def shards(
    features,
    tile_vals,
    tile_rows,
    tile_cols,
    tile_count,
    cut_weights,
    send_idx,
    send_count,
    weight,
    bias,
    cotangent,
):
    rows_dev, feature_width = features.shape
    tile_side = tile_vals.shape[1]
    blk_size = lax.axis_size("blk")
    dom_size = lax.axis_size("dom")
    position = lax.axis_index("blk")
    row_blocks = rows_dev // tile_side
    slot_count = tile_vals.shape[0] // blk_size
    send_most = send_idx.shape[1] // dom_size
    tiles = tile_vals.reshape(blk_size, slot_count, tile_side, tile_side)
    row_ids = tile_rows.reshape(blk_size, slot_count)
    col_ids = tile_cols.reshape(blk_size, slot_count)
    counts = tile_count.reshape(blk_size)
    slot_ids = jnp.arange(slot_count, dtype=jnp.int32)
    live_all = slot_ids[None, :] < counts[:, None]
    sent_rows = send_idx.reshape(dom_size * send_most)
    sent_live = (
        jnp.arange(send_most, dtype=jnp.int32)[None, :] < send_count.reshape(dom_size)[:, None]
    )
    outgoing = jnp.take(features, sent_rows, axis=0).reshape(dom_size, send_most, feature_width)
    outgoing = jnp.where(sent_live[:, :, None], outgoing, jnp.zeros_like(outgoing))
    received = lax.all_to_all(outgoing, "dom", split_axis=0, concat_axis=0, tiled=True)
    cut_part = jnp.dot(
        cut_weights,
        received.reshape(dom_size * send_most, feature_width),
        preferred_element_type=jnp.float32,
    )
    empty = jnp.zeros((row_blocks, tile_side, feature_width), jnp.float32)
    piece = lax.all_gather(features, "blk", axis=0, tiled=True)
    start = jnp.int32(0)
    piece_rows = piece.shape[0]
    padded = pad_piece(piece, tile_side)

    def one_step(source_step, partial_value):
        source = (position - source_step) % blk_size
        lowest = source * rows_dev
        touches = (lowest < start + piece_rows) & (lowest + rows_dev > start)

        def work(inner):
            firsts = lowest + col_ids[source_step] * tile_side
            picked, inside = pick_blocks(padded, piece_rows, firsts, tile_side)
            return accumulate(
                inner,
                tiles[source_step],
                picked,
                row_ids[source_step],
                inside & live_all[source_step],
                False,
            )

        return lax.cond(touches, work, lambda inner: inner, partial_value)

    intra = lax.fori_loop(0, blk_size, one_step, empty).reshape(rows_dev, feature_width)
    aggregated = (intra + cut_part).astype(jnp.bfloat16)
    pre = jnp.dot(aggregated, weight, preferred_element_type=jnp.float32) + bias
    sigmoid_pre = jax.nn.sigmoid(pre)
    out_y = (pre * sigmoid_pre).astype(jnp.bfloat16)
    dpre = (cotangent.astype(jnp.float32) * sigmoid_pre * (1.0 + pre * (1.0 - sigmoid_pre))).astype(
        jnp.bfloat16
    )
    weight_term = lax.dot_general(
        aggregated, dpre, (((0,), (0,)), ((), ())), preferred_element_type=jnp.float32
    )
    bias_term = jnp.sum(dpre.astype(jnp.float32), axis=0)
    dz_rows = lax.dot_general(
        dpre, weight, (((1,), (1,)), ((), ())), preferred_element_type=jnp.float32
    ).astype(jnp.bfloat16)
    cut_back = lax.dot_general(
        cut_weights, dz_rows, (((0,), (0,)), ((), ())), preferred_element_type=jnp.float32
    ).astype(jnp.bfloat16)
    returned = lax.all_to_all(
        cut_back.reshape(dom_size, send_most, feature_width),
        "dom",
        split_axis=0,
        concat_axis=0,
        tiled=True,
    )
    returned = jnp.where(sent_live[:, :, None], returned.astype(jnp.float32), 0.0)
    cut_grad = (
        jnp.zeros((rows_dev, feature_width), jnp.float32)
        .at[sent_rows]
        .add(returned.reshape(dom_size * send_most, feature_width))
    )
    dz_blocks = dz_rows.reshape(row_blocks, tile_side, feature_width)
    row_total = rows_dev * lax.axis_size("blk")

    def one_panel(panel_idx):
        source_step = (position - panel_idx) % blk_size
        picked = jnp.take(dz_blocks, row_ids[source_step], axis=0)
        return accumulate(
            empty, tiles[source_step], picked, col_ids[source_step], live_all[source_step], True
        )

    panel_ids = jnp.arange(row_total // rows_dev, dtype=jnp.int32)
    intra_grad = lax.psum_scatter(
        lax.map(one_panel, panel_ids).reshape(row_total, feature_width),
        "blk",
        scatter_dimension=0,
        tiled=True,
    )
    weight_sum, bias_sum = lax.psum((weight_term, bias_term), ("dom", "blk"))
    scale = 1.0 / math.sqrt(dom_size * blk_size * rows_dev)
    grad_x = (intra_grad + cut_grad).astype(jnp.bfloat16)
    return (out_y, grad_x, weight_sum * scale, bias_sum * scale)


def solution(mesh):
    in_specs = (
        P(("dom", "blk"), None),
        P(("dom", "blk"), None, None),
        P(("dom", "blk"), None),
        P(("dom", "blk"), None),
        P(("dom", "blk"), None),
        P(("dom", "blk"), None),
        P(("dom", "blk"), None),
        P(("dom", "blk"), None),
        P(),
        P(),
        P(("dom", "blk"), None),
    )
    out_specs = (P(("dom", "blk"), None), P(("dom", "blk"), None), P(), P())
    return jax.shard_map(shards, mesh=mesh, in_specs=in_specs, out_specs=out_specs, check_vma=False)
```

profile of v0, /device:TPU:0, one launch (start us, length us, event | category | flops | bytes accessed | tf_op | source)
XLA Modules:
  0.0 325.4 jit_solution(1108997307019440022)
XLA Ops:
  9.4 2.2 gather_fusion.1
  13.1 5.2 %all-to-all-start = ((bf16[8,48,128]{2,1,0:T(8,128)(2,1)}), bf16[8,48,128]{2,1,0:T(8,128)(2,1)S(1)}, u32[]{:S(2)}, u32[]{:S(2)}) async-start(bf16[8,48,128]{2,1,0:T(8,128)(2,1)} %select_select_fusion), calls=%async_computation | async-start | bytes 196608 | tf_op jit(solution)/shard_map/all_to_all | solution.py:66
  22.4 17.8 %all-gather.2.cloned.1.call-done = bf16[4096,128]{1,0:T(8,128)(2,1)} async-done(((bf16[1024,128]{1,0:T(8,128)(2,1)}), bf16[4096,128]{1,0:T(8,128)(2,1)}) %all-gather.2.cloned.1.call-update) | async-done | bytes 1048592 | tf_op jit(solution)/shard_map/all_gather | solution.py:73
  41.6 99.8 %while.34 = (s32[]{:T(128)}, f32[8,128,128]{1,0,2:T(8,128)S(1)}, s32[]{:T(128)}, s32[4,18]{1,0:T(4,128)S(1)}, bf16[4352,128]{1,0:T(8,128)(2,1)S(1)}, /*index=5*/...) while((s32[]{:T(128)}, f32[8,128,128]{1,0,2:T(8,128)S(1)}, ...), condition=%wide.region_3.4_spmd.clone, body=%wide.region_0.3_spmd.clone.sunk | while | flops 80347744 | bytes 3475381 | solution.py:97
  41.7 24.9 %conditional.3 = (f32[8,128,128]{1,0,2:T(8,128)S(1)}) conditional(s32[]{:T(128)} %convert_element_type.66, f32[8,128,128]{1,0,2:T(8,128)S(1)} %get-tuple-element.590, (s32[]{:T(128)}, s32[]{:T(128)}, s32[4,18]{1,0:T(4,128)S(1)}, bf16[4352,128]{1,0:T(8,128)(2,1)S(1)}, bf16[4,18,128,128]{3,2,1,0:T(8,128)(2,1)}, /*index=5*/s32[4,18]{1,0:T(4,128)S(1)}, ...), branch_computations={%region_1.1_spmd, %region_2.2_spmd} | conditional | flops 80347728 | bytes 3474709 | solution.py:95
  41.9 22.6 %while.32 = (s32[]{:T(128)}, bf16[4352,128]{1,0:T(8,128)(2,1)S(1)}, s32[18,2]{0,1:T(2,128)S(1)}, bf16[18,128,128]{2,1,0:T(8,128)(2,1)S(1)}, s32[]{:T(128)}) while((s32[]{:T(128)}, bf16[4352,128]{1,0:T(8,128)(2,1)S(1)}, s32[18,2]{0,1:T(2,128)S(1)}, bf16[18,128,128]{2,1,0:T(8,128)(2,1)S(1)}, s32[]{:T(128)}) %tuple.94), condition=%wide.while_cond, body=%wide.while_body.sunk | while | flops 2 | bytes 65641 | solution.py:15
  64.5 1.6 fusion.10
  66.6 24.9 %conditional.3 = (f32[8,128,128]{1,0,2:T(8,128)S(1)}) conditional(s32[]{:T(128)} %convert_element_type.66, f32[8,128,128]{1,0,2:T(8,128)S(1)} %get-tuple-element.590, (s32[]{:T(128)}, s32[]{:T(128)}, s32[4,18]{1,0:T(4,128)S(1)}, bf16[4352,128]{1,0:T(8,128)(2,1)S(1)}, bf16[4,18,128,128]{3,2,1,0:T(8,128)(2,1)}, /*index=5*/s32[4,18]{1,0:T(4,128)S(1)}, ...), branch_computations={%region_1.1_spmd, %region_2.2_spmd} | conditional | flops 80347728 | bytes 3474709 | solution.py:95
  66.8 22.6 %while.32 = (s32[]{:T(128)}, bf16[4352,128]{1,0:T(8,128)(2,1)S(1)}, s32[18,2]{0,1:T(2,128)S(1)}, bf16[18,128,128]{2,1,0:T(8,128)(2,1)S(1)}, s32[]{:T(128)}) while((s32[]{:T(128)}, bf16[4352,128]{1,0:T(8,128)(2,1)S(1)}, s32[18,2]{0,1:T(2,128)S(1)}, bf16[18,128,128]{2,1,0:T(8,128)(2,1)S(1)}, s32[]{:T(128)}) %tuple.94), condition=%wide.while_cond, body=%wide.while_body.sunk | while | flops 2 | bytes 65641 | solution.py:15
  89.4 1.6 fusion.10
  91.6 24.9 %conditional.3 = (f32[8,128,128]{1,0,2:T(8,128)S(1)}) conditional(s32[]{:T(128)} %convert_element_type.66, f32[8,128,128]{1,0,2:T(8,128)S(1)} %get-tuple-element.590, (s32[]{:T(128)}, s32[]{:T(128)}, s32[4,18]{1,0:T(4,128)S(1)}, bf16[4352,128]{1,0:T(8,128)(2,1)S(1)}, bf16[4,18,128,128]{3,2,1,0:T(8,128)(2,1)}, /*index=5*/s32[4,18]{1,0:T(4,128)S(1)}, ...), branch_computations={%region_1.1_spmd, %region_2.2_spmd} | conditional | flops 80347728 | bytes 3474709 | solution.py:95
  91.7 22.6 %while.32 = (s32[]{:T(128)}, bf16[4352,128]{1,0:T(8,128)(2,1)S(1)}, s32[18,2]{0,1:T(2,128)S(1)}, bf16[18,128,128]{2,1,0:T(8,128)(2,1)S(1)}, s32[]{:T(128)}) while((s32[]{:T(128)}, bf16[4352,128]{1,0:T(8,128)(2,1)S(1)}, s32[18,2]{0,1:T(2,128)S(1)}, bf16[18,128,128]{2,1,0:T(8,128)(2,1)S(1)}, s32[]{:T(128)}) %tuple.94), condition=%wide.while_cond, body=%wide.while_body.sunk | while | flops 2 | bytes 65641 | solution.py:15
  114.4 1.6 fusion.10
  116.5 24.9 %conditional.3 = (f32[8,128,128]{1,0,2:T(8,128)S(1)}) conditional(s32[]{:T(128)} %convert_element_type.66, f32[8,128,128]{1,0,2:T(8,128)S(1)} %get-tuple-element.590, (s32[]{:T(128)}, s32[]{:T(128)}, s32[4,18]{1,0:T(4,128)S(1)}, bf16[4352,128]{1,0:T(8,128)(2,1)S(1)}, bf16[4,18,128,128]{3,2,1,0:T(8,128)(2,1)}, /*index=5*/s32[4,18]{1,0:T(4,128)S(1)}, ...), branch_computations={%region_1.1_spmd, %region_2.2_spmd} | conditional | flops 80347728 | bytes 3474709 | solution.py:95
  116.7 22.6 %while.32 = (s32[]{:T(128)}, bf16[4352,128]{1,0:T(8,128)(2,1)S(1)}, s32[18,2]{0,1:T(2,128)S(1)}, bf16[18,128,128]{2,1,0:T(8,128)(2,1)S(1)}, s32[]{:T(128)}) while((s32[]{:T(128)}, bf16[4352,128]{1,0:T(8,128)(2,1)S(1)}, s32[18,2]{0,1:T(2,128)S(1)}, bf16[18,128,128]{2,1,0:T(8,128)(2,1)S(1)}, s32[]{:T(128)}) %tuple.94), condition=%wide.while_cond, body=%wide.while_body.sunk | while | flops 2 | bytes 65641 | solution.py:15
  139.3 1.6 fusion.10
  141.8 2.5 convert_reduce_fusion
  145.6 20.2 %while.33 = (s32[]{:T(128)}, f32[4,8,128,128]{3,2,1,0:T(8,128)}, s32[4]{0:T(128)S(1)}, s32[]{:T(128)}, s32[4,18]{1,0:T(4,128)S(1)}, /*index=5*/bf16[8,128,128]{2...) while((s32[]{:T(128)}, f32[4,8,128,128]{3,2,1,0:T(8,128)}, ...), condition=%wide.region_5.6_spmd, body=%wide.region_4.5_spmd.sunk | while | flops 80512464 | bytes 6165470 | solution.py:140
  166.9 3.7 %all-to-all-start.1 = ((bf16[8,48,128]{2,1,0:T(8,128)(2,1)}), bf16[8,48,128]{2,1,0:T(8,128)(2,1)S(1)}, u32[]{:S(2)}, u32[]{:S(2)}) async-start(bf16[8,48,128]{2,1,0:T(8,128)(2,1)} %bitcast.26), calls=%async_computation.2 | async-start | bytes 196608 | tf_op jit(solution)/shard_map/all_to_all | solution.py:115
  170.6 40.6 %psum.15 = f32[256]{0:T(256)S(1)} all-reduce(f32[256]{0:T(256)S(1)} %get-tuple-element.426), channel_id=1, replica_groups=mesh['dom'=8,'blk'=4] {'dom','blk'}, use_global_device_ids=true, to_apply=%region_10.11 | all-reduce | flops 256 | bytes 2048 | tf_op jit(solution)/shard_map/psum | solution.py:145
  211.7 56.0 %all-reduce.3.cloned.1.call-done = f32[128,256]{1,0:T(8,128)} async-done(((f32[128,256]{1,0:T(8,128)}), f32[128,256]{1,0:T(8,128)}) %all-reduce.3.cloned.1.call-update) | async-done | bytes 131088 | tf_op jit(solution)/shard_map/psum | solution.py:145
  269.4 43.5 %reduce-scatter.2.cloned.1.call-done = f32[1024,128]{1,0:T(8,128)} async-done(((f32[4096,128]{1,0:T(8,128)}), f32[1024,128]{1,0:T(8,128)}) %reduce-scatter.2.cloned.1.call-update) | async-done | bytes 524304 | tf_op jit(solution)/shard_map/reduce_scatter | solution.py:139
  312.9 4.2 %scatter_fusion = f32[1024,128]{1,0:T(8,128)} fusion(f32[1024,128]{1,0:T(8,128)} %reduce-scatter.2.cloned.1.call-done, s32[384]{0:T(512)S(1)} %fusion.45, f32[384,128]{1,0:T(8,128)S(1)} %bitcast.102), kind=kCustom, calls=%fused_computation.2 | custom fusion | flops 49152 | bytes 591360 | tf_op jit(solution)/shard_map/scatter-add | solution.py:126
  317.1 1.8 convert_element_type.50
  (333 shorter events, 122.7 us)
Async XLA Ops:
  7.2 134.2 %copy-start = (bf16[1024,384]{1,0:T(8,128)(2,1)S(1)}, bf16[1024,384]{1,0:T(8,128)(2,1)}, u32[]{:S(2)}) copy-start(bf16[1024,384]{1,0:T(8,128)(2,1)} %param.22) | copy-start | bytes 2359300
  7.2 33.1 %all-gather.2.cloned.1.call-start = ((), (), s32[]{:S(2)}) async-start(), calls=%async_computation.3 | async-start | bytes 1310720 | tf_op jit(solution)/shard_map/all_gather | solution.py:73
  7.9 33.7 %copy-start.2 = (s32[1,4]{1,0:T(1,128)S(1)}, s32[1,4]{1,0:T(1,128)}, u32[]{:S(2)}) copy-start(s32[1,4]{1,0:T(1,128)} %param.21) | copy-start | bytes 52
  13.1 128.3 %all-to-all-start = ((bf16[8,48,128]{2,1,0:T(8,128)(2,1)}), bf16[8,48,128]{2,1,0:T(8,128)(2,1)S(1)}, u32[]{:S(2)}, u32[]{:S(2)}) async-start(bf16[8,48,128]{2,1,0:T(8,128)(2,1)} %select_select_fusion), calls=%async_computation | async-start | bytes 196608 | tf_op jit(solution)/shard_map/all_to_all | solution.py:66
  18.3 249.4 %all-reduce.3.cloned.1.call-start = ((), (), s32[]{:S(2)}) async-start(), calls=%async_computation.5 | async-start | bytes 262144 | tf_op jit(solution)/shard_map/psum | solution.py:145
  41.6 100.2 %copy-start.1 = (bf16[128,256]{1,0:T(8,128)(2,1)S(1)}, bf16[128,256]{1,0:T(8,128)(2,1)}, u32[]{:S(2)}) copy-start(bf16[128,256]{1,0:T(8,128)(2,1)} %param.25) | copy-start | bytes 196612
  41.6 100.2 %copy-start.3 = (f32[256]{0:T(256)S(1)}, f32[256]{0:T(256)}, u32[]{:S(2)}) copy-start(f32[256]{0:T(256)} %param.26) | copy-start | bytes 3076
  145.6 167.3 %reduce-scatter.2.cloned.1.call-start = ((), (), s32[]{:S(2)}) async-start(), calls=%async_computation.4 | async-start | bytes 2621440 | tf_op jit(solution)/shard_map/reduce_scatter | solution.py:139
  166.9 102.3 %all-to-all-start.1 = ((bf16[8,48,128]{2,1,0:T(8,128)(2,1)}), bf16[8,48,128]{2,1,0:T(8,128)(2,1)S(1)}, u32[]{:S(2)}, u32[]{:S(2)}) async-start(bf16[8,48,128]{2,1,0:T(8,128)(2,1)} %bitcast.26), calls=%async_computation.2 | async-start | bytes 196608 | tf_op jit(solution)/shard_map/all_to_all | solution.py:115
Sparse Core Ops, SparseCore 0:
  9.6 30.6 all-gather.1
  145.7 121.9 all-reduce.2
  270.0 42.8 reduce-scatter.1
where the time goes:
time: 327 us; the launch traced here: 325 us
  waiting for transfers between devices  118 us (36%)
  local copies, waits for them, and re-layouts  102 us (31%)
  blocking collectives  40.6 us (12%)
  matrix products  20.5 us (6%)
  other arithmetic  16.4 us (5%)
  between operations  13.9 us (4%)
  starting transfers between devices  8.96 us (3%)
  loops' own time  4.92 us (2%)
    gather x216, local copies, waits for them, and re-layouts  89 us
    psum x1, waiting for transfers between devices, shards(): weight_sum, bias_sum = lax.psum((weight_term, bias_term), ('dom', 'blk'))  56 us
    reduce_scatter x1, waiting for transfers between devices, shards(): lax.psum_scatter(lax.map(one_panel, panel_ids).reshape(row_total, feature...  43.5 us
    psum x1, blocking collectives, shards(): weight_sum, bias_sum = lax.psum((weight_term, bias_term), ('dom', 'blk'))  40.6 us
    all_gather x1, waiting for transfers between devices, shards(): piece = lax.all_gather(features, 'blk', axis=0, tiled=True)  17.8 us
    dot_general x16, matrix products, accumulate(): jnp.einsum(pattern, selector, tiles_here, picked, preferred_element_type=...  16 us
  transfers between devices with their start and end apart: 5, of which 3 were waited for; matrix products, arithmetic and copies ran while one was open for 40% of the time, Pallas kernels for 0%

commit v1 on v0

--- a/solution.py
+++ b/solution.py
@@ -70,7 +70,21 @@
         preferred_element_type=jnp.float32,
     )
     empty = jnp.zeros((row_blocks, tile_side, feature_width), jnp.float32)
-    piece = lax.all_gather(features, "blk", axis=0, tiled=True)
+    ways, here, step = (lax.axis_size("blk"), lax.axis_index("blk"), features.shape[0])
+    shape = [n * ways if d == 0 else n for d, n in enumerate(features.shape)]
+    full = lax.dynamic_update_slice_in_dim(
+        jnp.zeros(shape, features.dtype), features, here * step, axis=0
+    )
+    going_up = going_down = features
+    for far in range(1, ways // 2 + 1):
+        going_up = lax.ppermute(going_up, "blk", [(d, (d + 1) % ways) for d in range(ways)])
+        full = lax.dynamic_update_slice_in_dim(full, going_up, (here - far) % ways * step, axis=0)
+        if 2 * far < ways:
+            going_down = lax.ppermute(going_down, "blk", [(d, (d - 1) % ways) for d in range(ways)])
+            full = lax.dynamic_update_slice_in_dim(
+                full, going_down, (here + far) % ways * step, axis=0
+            )
+    piece = full
     start = jnp.int32(0)
     piece_rows = piece.shape[0]
     padded = pad_piece(piece, tile_side)

time: 327 us -> 304 us (0.930)
  waiting for transfers between devices: 118 us -> 83.3 us
  local copies, waits for them, and re-layouts: 102 us -> 108 us
  starting transfers between devices: 8.96 us -> 13.1 us
    reduce_scatter x1, waiting for transfers between devices: 43.5 us -> 0.03 us  [shards(): lax.psum_scatter(lax.map(one_panel, panel_ids).reshape(row_total, feature...]
    psum x1, waiting for transfers between devices: 56 us -> 75.2 us  [shards(): weight_sum, bias_sum = lax.psum((weight_term, bias_term), ('dom', 'blk'))]
    all_gather x1 -> x0, waiting for transfers between devices: 17.8 us -> none  [shards(): piece = lax.all_gather(features, 'blk', axis=0, tiled=True)]
    ppermute x0 -> x3, waiting for transfers between devices: none -> 7.96 us  [the longest x2 7.96 us: shards(): lax.ppermute(going_up, 'blk', [(d, (d + 1) % ways) for d in range(ways)])]
    gather x216, local copies, waits for them, and re-layouts: 89 us -> 94.5 us
    ppermute x0 -> x3, starting transfers between devices: none -> 5.17 us  [the longest x2 3.08 us: shards(): lax.ppermute(going_up, 'blk', [(d, (d + 1) % ways) for d in range(ways)])]
  transfers between devices with their start and end apart: 5 -> 7, of which waited for: 3 -> 2; matrix products, arithmetic and copies ran while one was open for 40% -> 44% of each run, Pallas kernels for 0% -> 0%
where the time goes in v1:
time: 304 us; the launch traced here: 302 us
  local copies, waits for them, and re-layouts  108 us (36%)
  waiting for transfers between devices  83.3 us (27%)
  blocking collectives  41.8 us (14%)
  matrix products  21.4 us (7%)
  between operations  15.8 us (5%)
  other arithmetic  13.9 us (5%)
  starting transfers between devices  13.1 us (4%)
  loops' own time  4.91 us (2%)
    gather x216, local copies, waits for them, and re-layouts  94.5 us
    psum x1, waiting for transfers between devices, shards(): weight_sum, bias_sum = lax.psum((weight_term, bias_term), ('dom', 'blk'))  75.2 us
    psum x1, blocking collectives, shards(): weight_sum, bias_sum = lax.psum((weight_term, bias_term), ('dom', 'blk'))  41.8 us
    dot_general x16, matrix products, accumulate(): jnp.einsum(pattern, selector, tiles_here, picked, preferred_element_type=...  16.1 us
    ppermute x2, waiting for transfers between devices, shards(): lax.ppermute(going_up, 'blk', [(d, (d + 1) % ways) for d in range(ways)])  7.96 us
  transfers between devices with their start and end apart: 7, of which 2 were waited for; matrix products, arithmetic and copies ran while one was open for 44% of the time, Pallas kernels for 0%

profile of v1, /device:TPU:0, one launch (start us, length us, event | category | flops | bytes accessed | tf_op | source)
XLA Modules:
  0.0 302.1 jit_solution(15436064767315982844)
XLA Ops:
  8.0 3.1 %collective-permute-start = (bf16[1024,128]{1,0:T(8,128)(2,1)}, bf16[1024,128]{1,0:T(8,128)(2,1)S(1)}, u32[]{:S(2)}, u32[]{:S(2)}) collective-permute-start(bf16[1024,128]{1,0:T(8,128)(2,1)} %param.17), channel_id=1, source_target_pairs={{0,1},{1,2},{2,3},{3,0},{4,5},{5,6},{6,7},{7,4},{8,9},{9,10},{10,1... | collective-permute-start | bytes 786440 | tf_op jit(solution)/shard_map/ppermute | solution.py:80
  11.1 2.1 collective-permute-start.1
  14.7 2.2 gather_fusion.1
  18.4 4.0 %all-to-all-start = ((bf16[8,48,128]{2,1,0:T(8,128)(2,1)}), bf16[8,48,128]{2,1,0:T(8,128)(2,1)}, u32[]{:S(2)}, u32[]{:S(2)}) async-start(bf16[8,48,128]{2,1,0:T(8,128)(2,1)} %select_select_fusion), calls=%async_computation | async-start | bytes 196608 | tf_op jit(solution)/shard_map/all_to_all | solution.py:66
  25.6 8.0 %collective-permute-done.2 = bf16[1024,128]{1,0:T(8,128)(2,1)S(1)} collective-permute-done((bf16[1024,128]{1,0:T(8,128)(2,1)S(1)}, bf16[1024,128]{1,0:T(8,128)(2,1)S(1)}, u32[]{:S(2)}, u32[]{:S(2)}) %collective-permute-start.2) | collective-permute-done | bytes 262176 | tf_op jit(solution)/shard_map/ppermute | solution.py:80
  33.8 105.3 %while.34 = (s32[]{:T(128)}, f32[8,128,128]{1,0,2:T(8,128)S(1)}, s32[]{:T(128)}, s32[4,18]{1,0:T(4,128)S(1)}, bf16[4352,128]{1,0:T(8,128)(2,1)S(1)}, /*index=5*/...) while((s32[]{:T(128)}, f32[8,128,128]{1,0,2:T(8,128)S(1)}, ...), condition=%wide.region_3.4_spmd.clone, body=%wide.region_0.3_spmd.clone.sunk | while | flops 80347744 | bytes 3475365 | solution.py:111
  33.8 26.3 %conditional.3 = (f32[8,128,128]{1,0,2:T(8,128)S(1)}) conditional(s32[]{:T(128)} %convert_element_type.66, f32[8,128,128]{1,0,2:T(8,128)S(1)} %get-tuple-element.590, (s32[]{:T(128)}, s32[]{:T(128)}, s32[4,18]{1,0:T(4,128)S(1)}, bf16[4352,128]{1,0:T(8,128)(2,1)S(1)}, bf16[4,18,128,128]{3,2,1,0:T(8,128)(2,1)}, /*index=5*/s32[4,18]{1,0:T(4,128)S(1)}, ...), branch_computations={%region_1.1_spmd, %region_2.2_spmd} | conditional | flops 80347728 | bytes 3474701 | solution.py:109
  33.9 24.0 %while.32 = (s32[]{:T(128)}, bf16[4352,128]{1,0:T(8,128)(2,1)S(1)}, s32[18,2]{0,1:T(2,128)S(1)}, bf16[18,128,128]{2,1,0:T(8,128)(2,1)S(1)}, s32[]{:T(128)}) while((s32[]{:T(128)}, bf16[4352,128]{1,0:T(8,128)(2,1)S(1)}, s32[18,2]{0,1:T(2,128)S(1)}, bf16[18,128,128]{2,1,0:T(8,128)(2,1)S(1)}, s32[]{:T(128)}) %tuple.94), condition=%wide.while_cond, body=%wide.while_body.sunk | while | flops 2 | bytes 65633 | solution.py:15
  60.1 26.3 %conditional.3 = (f32[8,128,128]{1,0,2:T(8,128)S(1)}) conditional(s32[]{:T(128)} %convert_element_type.66, f32[8,128,128]{1,0,2:T(8,128)S(1)} %get-tuple-element.590, (s32[]{:T(128)}, s32[]{:T(128)}, s32[4,18]{1,0:T(4,128)S(1)}, bf16[4352,128]{1,0:T(8,128)(2,1)S(1)}, bf16[4,18,128,128]{3,2,1,0:T(8,128)(2,1)}, /*index=5*/s32[4,18]{1,0:T(4,128)S(1)}, ...), branch_computations={%region_1.1_spmd, %region_2.2_spmd} | conditional | flops 80347728 | bytes 3474701 | solution.py:109
  60.2 24.0 %while.32 = (s32[]{:T(128)}, bf16[4352,128]{1,0:T(8,128)(2,1)S(1)}, s32[18,2]{0,1:T(2,128)S(1)}, bf16[18,128,128]{2,1,0:T(8,128)(2,1)S(1)}, s32[]{:T(128)}) while((s32[]{:T(128)}, bf16[4352,128]{1,0:T(8,128)(2,1)S(1)}, s32[18,2]{0,1:T(2,128)S(1)}, bf16[18,128,128]{2,1,0:T(8,128)(2,1)S(1)}, s32[]{:T(128)}) %tuple.94), condition=%wide.while_cond, body=%wide.while_body.sunk | while | flops 2 | bytes 65633 | solution.py:15
  84.2 1.6 fusion.10
  86.4 26.3 %conditional.3 = (f32[8,128,128]{1,0,2:T(8,128)S(1)}) conditional(s32[]{:T(128)} %convert_element_type.66, f32[8,128,128]{1,0,2:T(8,128)S(1)} %get-tuple-element.590, (s32[]{:T(128)}, s32[]{:T(128)}, s32[4,18]{1,0:T(4,128)S(1)}, bf16[4352,128]{1,0:T(8,128)(2,1)S(1)}, bf16[4,18,128,128]{3,2,1,0:T(8,128)(2,1)}, /*index=5*/s32[4,18]{1,0:T(4,128)S(1)}, ...), branch_computations={%region_1.1_spmd, %region_2.2_spmd} | conditional | flops 80347728 | bytes 3474701 | solution.py:109
  86.5 24.0 %while.32 = (s32[]{:T(128)}, bf16[4352,128]{1,0:T(8,128)(2,1)S(1)}, s32[18,2]{0,1:T(2,128)S(1)}, bf16[18,128,128]{2,1,0:T(8,128)(2,1)S(1)}, s32[]{:T(128)}) while((s32[]{:T(128)}, bf16[4352,128]{1,0:T(8,128)(2,1)S(1)}, s32[18,2]{0,1:T(2,128)S(1)}, bf16[18,128,128]{2,1,0:T(8,128)(2,1)S(1)}, s32[]{:T(128)}) %tuple.94), condition=%wide.while_cond, body=%wide.while_body.sunk | while | flops 2 | bytes 65633 | solution.py:15
  110.5 1.6 fusion.10
  112.8 26.3 %conditional.3 = (f32[8,128,128]{1,0,2:T(8,128)S(1)}) conditional(s32[]{:T(128)} %convert_element_type.66, f32[8,128,128]{1,0,2:T(8,128)S(1)} %get-tuple-element.590, (s32[]{:T(128)}, s32[]{:T(128)}, s32[4,18]{1,0:T(4,128)S(1)}, bf16[4352,128]{1,0:T(8,128)(2,1)S(1)}, bf16[4,18,128,128]{3,2,1,0:T(8,128)(2,1)}, /*index=5*/s32[4,18]{1,0:T(4,128)S(1)}, ...), branch_computations={%region_1.1_spmd, %region_2.2_spmd} | conditional | flops 80347728 | bytes 3474701 | solution.py:109
  112.8 24.0 %while.32 = (s32[]{:T(128)}, bf16[4352,128]{1,0:T(8,128)(2,1)S(1)}, s32[18,2]{0,1:T(2,128)S(1)}, bf16[18,128,128]{2,1,0:T(8,128)(2,1)S(1)}, s32[]{:T(128)}) while((s32[]{:T(128)}, bf16[4352,128]{1,0:T(8,128)(2,1)S(1)}, s32[18,2]{0,1:T(2,128)S(1)}, bf16[18,128,128]{2,1,0:T(8,128)(2,1)S(1)}, s32[]{:T(128)}) %tuple.94), condition=%wide.while_cond, body=%wide.while_body.sunk | while | flops 2 | bytes 65633 | solution.py:15
  136.8 1.6 fusion.10
  140.4 2.5 convert_reduce_fusion
  144.2 20.2 %while.33 = (s32[]{:T(128)}, f32[4,8,128,128]{3,2,1,0:T(8,128)}, s32[4]{0:T(128)S(1)}, s32[]{:T(128)}, s32[4,18]{1,0:T(4,128)S(1)}, /*index=5*/bf16[8,128,128]{2...) while((s32[]{:T(128)}, f32[4,8,128,128]{3,2,1,0:T(8,128)}, ...), condition=%wide.region_5.6_spmd, body=%wide.region_4.5_spmd.sunk | while | flops 80512464 | bytes 6165970 | solution.py:154
  165.5 3.9 %all-to-all-start.1 = ((bf16[8,48,128]{2,1,0:T(8,128)(2,1)}), bf16[8,48,128]{2,1,0:T(8,128)(2,1)S(1)}, u32[]{:S(2)}, u32[]{:S(2)}) async-start(bf16[8,48,128]{2,1,0:T(8,128)(2,1)} %bitcast.26), calls=%async_computation.2 | async-start | bytes 196608 | tf_op jit(solution)/shard_map/all_to_all | solution.py:129
  169.3 41.8 %psum.15 = f32[256]{0:T(256)S(1)} all-reduce(f32[256]{0:T(256)S(1)} %get-tuple-element.426), channel_id=1, replica_groups=mesh['dom'=8,'blk'=4] {'dom','blk'}, use_global_device_ids=true, to_apply=%region_10.11 | all-reduce | flops 256 | bytes 2048 | tf_op jit(solution)/shard_map/psum | solution.py:159
  211.7 75.2 %all-reduce.3.cloned.1.call-done = f32[128,256]{1,0:T(8,128)} async-done(((f32[128,256]{1,0:T(8,128)}), f32[128,256]{1,0:T(8,128)}) %all-reduce.3.cloned.1.call-update) | async-done | bytes 131088 | tf_op jit(solution)/shard_map/psum | solution.py:159
  288.7 4.2 %scatter_fusion = f32[1024,128]{1,0:T(8,128)} fusion(f32[1024,128]{1,0:T(8,128)} %reduce-scatter.2.cloned.1.call-done, s32[384]{0:T(512)S(1)} %fusion.45, f32[384,128]{1,0:T(8,128)S(1)} %bitcast.102), kind=kCustom, calls=%fused_computation.2 | custom fusion | flops 49152 | bytes 591360 | tf_op jit(solution)/shard_map/scatter-add | solution.py:140
  292.9 1.8 convert_element_type.50
  (347 shorter events, 127.8 us)
Async XLA Ops:
  8.0 131.1 %copy-start = (bf16[1024,384]{1,0:T(8,128)(2,1)S(1)}, bf16[1024,384]{1,0:T(8,128)(2,1)}, u32[]{:S(2)}) copy-start(bf16[1024,384]{1,0:T(8,128)(2,1)} %param.22) | copy-start | bytes 2359300
  8.0 15.3 %copy-start.1 = (bf16[1024,128]{1,0:T(8,128)(2,1)S(1)}, bf16[1024,128]{1,0:T(8,128)(2,1)}, u32[]{:S(2)}) copy-start(bf16[1024,128]{1,0:T(8,128)(2,1)} %param.17) | copy-start | bytes 786436
  8.0 16.0 %copy-start.5 = (s32[1,72]{1,0:T(1,128)S(1)}, s32[1,72]{1,0:T(1,128)}, u32[]{:S(2)}) copy-start(s32[1,72]{1,0:T(1,128)} %param.20) | copy-start | bytes 868
  8.0 16.7 %copy-start.6 = (s32[1,72]{1,0:T(1,128)S(1)}, s32[1,72]{1,0:T(1,128)}, u32[]{:S(2)}) copy-start(s32[1,72]{1,0:T(1,128)} %param.19) | copy-start | bytes 868
  8.0 15.1 %collective-permute-start = (bf16[1024,128]{1,0:T(8,128)(2,1)}, bf16[1024,128]{1,0:T(8,128)(2,1)S(1)}, u32[]{:S(2)}, u32[]{:S(2)}) collective-permute-start(bf16[1024,128]{1,0:T(8,128)(2,1)} %param.17), channel_id=1, source_target_pairs={{0,1},{1,2},{2,3},{3,0},{4,5},{5,6},{6,7},{7,4},{8,9},{9,10},{10,1... | collective-permute-start | bytes 786440 | tf_op jit(solution)/shard_map/ppermute | solution.py:80
  11.1 14.4 %collective-permute-start.1 = (bf16[1024,128]{1,0:T(8,128)(2,1)}, bf16[1024,128]{1,0:T(8,128)(2,1)S(1)}, u32[]{:S(2)}, u32[]{:S(2)}) collective-permute-start(bf16[1024,128]{1,0:T(8,128)(2,1)} %param.17), channel_id=1, source_target_pairs={{0,3},{1,0},{2,1},{3,2},{4,7},{5,4},{6,5},{7,6},{8,11},{9,8},{10,9... | collective-permute-start | bytes 786440 | tf_op jit(solution)/shard_map/ppermute | solution.py:83
  18.4 120.6 %all-to-all-start = ((bf16[8,48,128]{2,1,0:T(8,128)(2,1)}), bf16[8,48,128]{2,1,0:T(8,128)(2,1)}, u32[]{:S(2)}, u32[]{:S(2)}) async-start(bf16[8,48,128]{2,1,0:T(8,128)(2,1)} %select_select_fusion), calls=%async_computation | async-start | bytes 196608 | tf_op jit(solution)/shard_map/all_to_all | solution.py:66
  22.4 264.6 %all-reduce.3.cloned.1.call-start = ((), (), s32[]{:S(2)}) async-start(), calls=%async_computation.4 | async-start | bytes 262144 | tf_op jit(solution)/shard_map/psum | solution.py:159
  23.2 10.4 %collective-permute-start.2 = (bf16[1024,128]{1,0:T(8,128)(2,1)S(1)}, bf16[1024,128]{1,0:T(8,128)(2,1)S(1)}, u32[]{:S(2)}, u32[]{:S(2)}) collective-permute-start(bf16[1024,128]{1,0:T(8,128)(2,1)S(1)} %collective-permute-done), channel_id=1, source_target_pairs={{0,1},{1,2},{2,3},{3,0},{4,5},{5,6},{6,7},{7,4},{8,9},{9,10},{10,1... | collective-permute-start | bytes 786440 | tf_op jit(solution)/shard_map/ppermute | solution.py:80
  25.5 8.2 %copy-start.3 = (s32[1,4]{1,0:T(1,128)S(1)}, s32[1,4]{1,0:T(1,128)}, u32[]{:S(2)}) copy-start(s32[1,4]{1,0:T(1,128)} %param.21) | copy-start | bytes 52
  33.7 106.6 %copy-start.2 = (bf16[128,256]{1,0:T(8,128)(2,1)S(1)}, bf16[128,256]{1,0:T(8,128)(2,1)}, u32[]{:S(2)}) copy-start(bf16[128,256]{1,0:T(8,128)(2,1)} %param.25) | copy-start | bytes 196612
  33.7 106.6 %copy-start.4 = (f32[256]{0:T(256)S(1)}, f32[256]{0:T(256)}, u32[]{:S(2)}) copy-start(f32[256]{0:T(256)} %param.26) | copy-start | bytes 3076
  144.1 144.6 %reduce-scatter.2.cloned.1.call-start = ((), (), s32[]{:S(2)}) async-start(), calls=%async_computation.3 | async-start | bytes 2621440 | tf_op jit(solution)/shard_map/reduce_scatter | solution.py:153
  165.5 123.1 %all-to-all-start.1 = ((bf16[8,48,128]{2,1,0:T(8,128)(2,1)}), bf16[8,48,128]{2,1,0:T(8,128)(2,1)S(1)}, u32[]{:S(2)}, u32[]{:S(2)}) async-start(bf16[8,48,128]{2,1,0:T(8,128)(2,1)} %bitcast.26), calls=%async_computation.2 | async-start | bytes 196608 | tf_op jit(solution)/shard_map/all_to_all | solution.py:129
Sparse Core Ops, SparseCore 0:
  144.2 142.6 all-reduce.2
Sparse Core Ops, SparseCore 1:
  164.5 43.1 reduce-scatter.1
